TPU v7x, 32 devices: a whole 2x2x4 slice. The times are simulated.
32 devices in a mesh: groups: 2 (over y), leaf: 8 (over z, x), probe: 2 (over core).
Axes of the slice: x: 2, y: 2, z: 4, core: 2. Of those that a mesh axis runs over, the one named last changes fastest.
Arguments:
- rhs: float32 [16, 32768], P('probe', ('groups', 'leaf')), parts along dimension 1, may hold values from -6 to 6
- points: float32 [3, 32768], P(None, ('groups', 'leaf')), parts along dimension 1, may hold values from 0 to 4, as said below
- basis: bfloat16 [320, 32768], P(None, ('groups', 'leaf')), parts along dimension 1
- tree_order: int32 [32768], P(('groups', 'leaf')), parts along dimension 0, may hold values from 0 to 16383, as said below
- lengthscale: float32 [2], P('groups'), parts along dimension 0, may hold values from 0.1 to 0.8
Outputs:
- solution: float32 [16, 32768], P('probe', ('groups', 'leaf')), parts along dimension 1
- residual: float32 [16, 32768], P('probe', ('groups', 'leaf')), parts along dimension 1
There are 2 independent parts, one for each index of `groups`. A program takes and returns all parts, laid end to end along the dimension named above; each array names one. Nothing has to cross between parts.
Inputs may be any that keep to these rules, and one draw needn't show every extreme that they name: `tree_order`: each block of 512 consecutive positions holds a permutation of that block's own positions. The 512 points of one leaf block lie in one unit cube.
All inputs are finite; a program needn't handle non-finite values.
Results may differ from a plain program's by a relative error of at most 0.034.
The roundings to bfloat16 on the way count: a program that leaves them out, or rounds other values in their place, can miss the bound.
Values sent between devices are 32-bit elements; how exact they have to be, the bound alone decides.
A program may use at most 64 MiB of HBM per device.

v0:
```python
import jax
import jax.numpy as jnp
from jax import lax
from jax.sharding import PartitionSpec as P

LEAF = 512
K = 64
ITERS = 4


NOISE = 0.5
ROOT_THREE = 1.7320508


def leaf_tile(coords, scale):
    offsets = coords[:, :, None] - coords[:, None, :]
    distance = jnp.sqrt(jnp.sum(offsets * offsets, axis=0))
    scaled = ROOT_THREE * distance / scale
    return ((1.0 + scaled) * jnp.exp(-scaled)).astype(jnp.bfloat16)


def build_tiles(points, scale):
    count = points.shape[1] // LEAF
    coords = jnp.transpose(points.reshape(3, count, LEAF), (1, 0, 2))
    return jax.vmap(lambda where: leaf_tile(where, scale))(coords)


def apply_tiles(low16, tiles):
    count = tiles.shape[0]
    blocks = low16.reshape(low16.shape[0], count, LEAF)
    near = jnp.einsum("rtn,tnm->rtm", blocks, tiles, preferred_element_type=jnp.float32)
    return near.reshape(low16.shape)


def squares(remain):
    return lax.psum(jnp.sum(remain * remain, axis=1, keepdims=True), "leaf")


def body(rhs, points, basis, tree_order, lengthscale):
    scale = lengthscale[0]
    here = lax.axis_index("leaf")
    span = rhs.shape[1]
    columns = rhs.shape[0]
    local_order = tree_order - here * span
    right = jnp.take(rhs, local_order, axis=1)
    cross = lax.axis_size("leaf").bit_length() - 1
    total = basis.shape[0] // K
    upper = basis[: cross * K]
    stored = build_tiles(points, scale)
    iterate = jnp.zeros_like(right)
    remain = right
    direction = right
    norm_now = squares(remain)
    for iteration in range(ITERS):
        operate_low16 = direction.astype(jnp.bfloat16)
        part_sums = lax.dot_general(
            operate_low16, upper, (((1,), (1,)), ((), ())), preferred_element_type=jnp.float32
        )
        piece = lax.all_gather(part_sums[None], "leaf", axis=0, tiled=True)
        rows = piece.shape[0]
        sender = jnp.arange(rows, dtype=jnp.int32)
        shifts = cross - jnp.arange(cross, dtype=jnp.int32)
        same = (
            jnp.right_shift(sender[None, :], shifts[:, None])
            == jnp.right_shift(here, shifts)[:, None]
        )
        weights = same.astype(jnp.float32)
        blocks = piece.reshape(rows, columns, cross, K)
        gathered = jnp.einsum("jd,drjk->rjk", weights, blocks, precision=lax.Precision.HIGHEST)
        node_sums = gathered.reshape(columns, cross * K)
        result = apply_tiles(operate_low16, stored) + NOISE * direction
        result = result + jnp.dot(
            node_sums.astype(jnp.bfloat16), upper, preferred_element_type=jnp.float32
        )
        for depth in range(cross, total):
            nodes = 2 ** (depth - cross)
            factor = basis[depth * K : (depth + 1) * K].reshape(K, nodes, span // nodes)
            pieces = operate_low16.reshape(columns, nodes, span // nodes)
            local_sums = jnp.einsum(
                "rmn,kmn->rmk", pieces, factor, preferred_element_type=jnp.float32
            )
            local_low = local_sums.astype(jnp.bfloat16)
            spread = jnp.einsum(
                "rmk,kmn->rmn", local_low, factor, preferred_element_type=jnp.float32
            )
            result = result + spread.reshape(columns, span)
        curve = lax.psum(jnp.sum(direction * result, axis=1, keepdims=True), "leaf")
        alpha = norm_now / curve
        iterate = iterate + alpha * direction
        remain = remain - alpha * result
        norm_next = squares(remain)
        direction = remain + norm_next / norm_now * direction
        norm_now = norm_next
    solution = jnp.zeros_like(iterate).at[:, local_order].set(iterate)
    residual = jnp.zeros_like(remain).at[:, local_order].set(remain)
    return (solution, residual)


def solution(mesh):
    in_specs = (
        P("probe", ("groups", "leaf")),
        P(None, ("groups", "leaf")),
        P(None, ("groups", "leaf")),
        P(("groups", "leaf")),
        P("groups"),
    )
    out_specs = (P("probe", ("groups", "leaf")), P("probe", ("groups", "leaf")))
    return jax.shard_map(body, mesh=mesh, in_specs=in_specs, out_specs=out_specs, check_vma=False)
```

profile of v0, /device:TPU:0, one launch (start us, length us, event | category | flops | bytes accessed | tf_op | source)
XLA Modules:
  0.0 340.6 jit_solution(16838094264774698215)
XLA Ops:
  0.6 0.7 compare_and_fusion
  1.4 1.3 copy.27
  2.6 5.5 %gather_fusion = f32[2048,8]{1,0:T(8,128)S(1)} fusion(f32[8,2048]{0,1:T(8,128)S(1)} %copy.27, s32[2048]{0:T(1024)S(1)} %broadcast_clamp_fusion), kind=kCustom, calls=%fused_computation | custom fusion | bytes 139264 | tf_op jit(solution)/shard_map/jit(_take)/gather | solution.py:45
  8.7 32.3 %all-gather = f32[64,192]{1,0:T(8,128)S(1)} all-gather(f32[8,192]{1,0:T(8,128)S(1)} %fusion.50), channel_id=2, replica_groups=mesh['groups'=2,'leaf'=8,'probe'=2] {'leaf'}, dimensions={0}, use_global_device_ids=true | all-gather | bytes 55296 | tf_op jit(solution)/shard_map/all_gather | solution.py:59
  41.5 0.7 convert_element_type.120
  42.8 1.9 multiply_reduce_fusion
  45.4 1.8 multiply_convert_fusion
  47.9 0.8 convolution_add_fusion.7
  48.8 0.7 slice.8
  49.5 2.0 fusion.11
  51.5 1.9 multiply_reduce_fusion.7
  53.4 21.9 %all-reduce = (f32[8,1]{0,1:T(1,128)}, f32[8,1]{0,1:T(1,128)}) all-reduce(f32[8,1]{0,1:T(1,128)} %bitcast.202, f32[8,1]{0,1:T(1,128)} %bitcast.201), channel_id=1, replica_groups=mesh['groups'=2,'leaf'=8,'probe'=2] {'leaf'}, use_global_device_ids=true, to_apply=%region_1.2 | all-reduce | flops 16 | bytes 128 | tf_op jit(solution)/shard_map/psum | solution.py:36
  76.6 0.7 multiply_reduce_fusion.6
  77.3 17.8 %psum.58 = f32[8,1]{0,1:T(1,128)} all-reduce(f32[8,1]{0,1:T(1,128)} %bitcast.205), channel_id=1, replica_groups=mesh['groups'=2,'leaf'=8,'probe'=2] {'leaf'}, use_global_device_ids=true, to_apply=%region_6.7 | all-reduce | flops 8 | bytes 64 | tf_op jit(solution)/shard_map/psum | solution.py:36
  95.8 0.9 fusion.88
  96.7 1.0 fusion.99
  98.0 32.5 %all-gather.1 = f32[64,192]{1,0:T(8,128)} all-gather(f32[8,192]{1,0:T(8,128)S(1)} %fusion.47), channel_id=3, replica_groups=mesh['groups'=2,'leaf'=8,'probe'=2] {'leaf'}, dimensions={0}, use_global_device_ids=true | all-gather | bytes 55296 | tf_op jit(solution)/shard_map/all_gather | solution.py:59
  130.5 1.6 reshape.174
  132.1 1.1 fusion.56
  133.9 1.4 convert_element_type.128
  135.2 1.7 convolution_add_fusion.5
  136.9 2.0 fusion.10
  138.9 2.6 multiply_reduce_fusion.5
  141.5 19.8 %psum.59 = f32[8,1]{0,1:T(1,128)} all-reduce(f32[8,1]{0,1:T(1,128)} %bitcast.206), channel_id=1, replica_groups=mesh['groups'=2,'leaf'=8,'probe'=2] {'leaf'}, use_global_device_ids=true, to_apply=%region_8.9 | all-reduce | flops 8 | bytes 64 | tf_op jit(solution)/shard_map/psum | solution.py:87
  161.3 0.7 divide_bitcast_fusion.4
  162.6 2.2 multiply_reduce_fusion.4
  164.8 17.7 %psum.60 = f32[8,1]{0,1:T(1,128)} all-reduce(f32[8,1]{0,1:T(1,128)} %bitcast.203), channel_id=1, replica_groups=mesh['groups'=2,'leaf'=8,'probe'=2] {'leaf'}, use_global_device_ids=true, to_apply=%region_10.11 | all-reduce | flops 8 | bytes 64 | tf_op jit(solution)/shard_map/psum | solution.py:36
  183.2 1.5 fusion.87
  184.7 1.0 fusion.100
  186.0 32.5 %all-gather.2 = f32[64,192]{1,0:T(8,128)} all-gather(f32[8,192]{1,0:T(8,128)S(1)} %fusion.44), channel_id=4, replica_groups=mesh['groups'=2,'leaf'=8,'probe'=2] {'leaf'}, dimensions={0}, use_global_device_ids=true | all-gather | bytes 55296 | tf_op jit(solution)/shard_map/all_gather | solution.py:59
  218.5 1.6 reshape.179
  220.1 1.1 fusion.54
  221.9 1.4 convert_element_type.135
  223.2 1.7 convolution_add_fusion.3
  224.9 2.0 fusion.9
  226.9 2.6 multiply_reduce_fusion.3
  229.6 19.8 %psum.61 = f32[8,1]{0,1:T(1,128)} all-reduce(f32[8,1]{0,1:T(1,128)} %bitcast.207), channel_id=1, replica_groups=mesh['groups'=2,'leaf'=8,'probe'=2] {'leaf'}, use_global_device_ids=true, to_apply=%region_12.13 | all-reduce | flops 8 | bytes 64 | tf_op jit(solution)/shard_map/psum | solution.py:87
  250.6 2.3 multiply_reduce_fusion.2
  252.9 17.8 %psum.62 = f32[8,1]{0,1:T(1,128)} all-reduce(f32[8,1]{0,1:T(1,128)} %bitcast.204), channel_id=1, replica_groups=mesh['groups'=2,'leaf'=8,'probe'=2] {'leaf'}, use_global_device_ids=true, to_apply=%region_14.15 | all-reduce | flops 8 | bytes 64 | tf_op jit(solution)/shard_map/psum | solution.py:36
  271.3 1.6 fusion.86
  272.8 1.0 fusion.101
  274.2 30.5 %all-gather.3 = f32[64,192]{1,0:T(8,128)S(1)} all-gather(f32[8,192]{1,0:T(8,128)S(1)} %fusion.41), channel_id=5, replica_groups=mesh['groups'=2,'leaf'=8,'probe'=2] {'leaf'}, dimensions={0}, use_global_device_ids=true | all-gather | bytes 55296 | tf_op jit(solution)/shard_map/all_gather | solution.py:59
  305.2 1.1 convolution_add_fusion.1
  307.1 19.1 %psum.63 = f32[8,1]{0,1:T(1,128)S(1)} all-reduce(f32[8,1]{0,1:T(1,128)S(1)} %bitcast.208), channel_id=1, replica_groups=mesh['groups'=2,'leaf'=8,'probe'=2] {'leaf'}, use_global_device_ids=true, to_apply=%region_16.17 | all-reduce | flops 8 | bytes 64 | tf_op jit(solution)/shard_map/psum | solution.py:87
  326.7 5.8 %scatter_custom_fusion.1 = f32[8,2048]{0,1:T(8,128)S(1)} fusion(s32[2048]{0:T(1024)S(1)} %get-tuple-element.23, f32[2048,8]{1,0:T(8,128)S(1)} %copy.40, f32[]{:T(128)} %constant.11.clone.1), kind=kCustom, calls=%fused_computation.33 | custom fusion | bytes 65540 | tf_op jit(solution)/shard_map/scatter | solution.py:95
  332.6 0.9 copy.42
  333.8 5.8 %scatter_custom_fusion = f32[8,2048]{0,1:T(8,128)S(1)} fusion(s32[2048]{0:T(1024)S(1)} %get-tuple-element.23, f32[2048,8]{1,0:T(8,128)S(1)} %copy.39, f32[]{:T(128)} %constant.11.clone.1), kind=kCustom, calls=%fused_computation.35 | custom fusion | bytes 65540 | tf_op jit(solution)/shard_map/scatter | solution.py:94
  339.7 0.9 copy.41
  (73 shorter events, 11.5 us)
Async XLA Ops:
  1.3 7.1 %copy-start = (bf16[320,2048]{1,0:T(8,128)(2,1)S(1)}, bf16[320,2048]{1,0:T(8,128)(2,1)}, u32[]{:S(2)}) copy-start(bf16[320,2048]{1,0:T(8,128)(2,1)} %param.7) | copy-start | bytes 3932164
  8.1 34.6 %copy-start.10 = (f32[3,2048]{1,0:T(4,128)S(1)}, f32[3,2048]{1,0:T(4,128)}, u32[]{:S(2)}) copy-start(f32[3,2048]{1,0:T(4,128)} %param.6) | copy-start | bytes 73732
  45.4 1.9 copy-start.12
  47.2 0.7 copy-start.11
  53.4 41.7 %copy-start.3 = (f32[8,2048]{1,0:T(8,128)}, f32[8,2048]{1,0:T(8,128)S(1)}, u32[]{:S(2)}) copy-start(f32[8,2048]{1,0:T(8,128)S(1)} %get-tuple-element.26) | copy-start | bytes 196612
  76.0 0.6 copy-start.13
  96.7 1.3 copy-start.7
  162.0 0.5 copy-start.15
  184.7 1.3 copy-start.8
  250.0 0.6 copy-start.17
  272.8 1.3 copy-start.5
  273.8 32.4 %copy-start.1 = (bf16[64,2048]{1,0:T(8,128)(2,1)S(1)}, bf16[64,2048]{1,0:T(8,128)(2,1)}, u32[]{:S(2)}) copy-start(bf16[64,2048]{1,0:T(8,128)(2,1)} %slice.8) | copy-start | bytes 786436
  273.8 32.7 %copy-start.4 = (f32[8,2048]{1,0:T(8,128)S(1)}, f32[8,2048]{1,0:T(8,128)}, u32[]{:S(2)}) copy-start(f32[8,2048]{1,0:T(8,128)} %get-tuple-element.13) | copy-start | bytes 196612
  304.7 1.6 copy-start.6
  304.8 21.4 %copy-start.19 = (f32[8,1]{0,1:T(1,128)S(1)}, f32[8,1]{0,1:T(1,128)}, u32[]{:S(2)}) copy-start(f32[8,1]{0,1:T(1,128)} %psum.62) | copy-start | bytes 100
  304.8 21.4 %copy-start.2 = (f32[8,2048]{1,0:T(8,128)S(1)}, f32[8,2048]{1,0:T(8,128)}, u32[]{:S(2)}) copy-start(f32[8,2048]{1,0:T(8,128)} %get-tuple-element.17) | copy-start | bytes 196612
  304.8 21.4 %copy-start.9 = (f32[8,2048]{1,0:T(8,128)S(1)}, f32[8,2048]{1,0:T(8,128)}, u32[]{:S(2)}) copy-start(f32[8,2048]{1,0:T(8,128)} %get-tuple-element.15) | copy-start | bytes 196612
  304.8 21.4 %copy-start.14 = (f32[8]{0:T(128)S(1)}, f32[8]{0:T(128)}, u32[]{:S(2)}) copy-start(f32[8]{0:T(128)} %copy-done.13) | copy-start | bytes 100
  304.8 21.4 %copy-start.16 = (f32[8]{0:T(128)S(1)}, f32[8]{0:T(128)}, u32[]{:S(2)}) copy-start(f32[8]{0:T(128)} %copy-done.15) | copy-start | bytes 100
  304.8 21.4 %copy-start.18 = (f32[8]{0:T(128)S(1)}, f32[8]{0:T(128)}, u32[]{:S(2)}) copy-start(f32[8]{0:T(128)} %copy-done.17) | copy-start | bytes 100
where the time goes:
time: 342 us; the launch traced here: 341 us
  blocking collectives  262 us (77%)
  local copies, waits for them, and re-layouts  32.8 us (10%)
  matrix products  26.6 us (8%)
  other arithmetic  17.9 us (5%)
    all_gather x4, blocking collectives, body(): piece = lax.all_gather(part_sums[None], 'leaf', axis=0, tiled=True)  128 us
    psum x4, blocking collectives, squares(): return lax.psum(jnp.sum(remain * remain, axis=1, keepdims=True), 'leaf')  75.2 us
    psum x3, blocking collectives, body(): curve = lax.psum(jnp.sum(direction * result, axis=1, keepdims=True), 'leaf')  58.7 us
    dot_general x8, matrix products, body(): jnp.einsum('rmk,kmn->rmn', local_low, factor, preferred_element_type=jnp....  13.9 us

commit v1 on v0

v1 whole, which is shorter than its diff:
```python
import functools

import jax
import jax.numpy as jnp
from jax import lax
from jax.experimental import pallas as pl
from jax.experimental.pallas import tpu as pltpu
from jax.sharding import PartitionSpec as P

LEAF = 512
K = 64
ITERS = 4
CHUNK = 128

NOISE = 0.5
ROOT_THREE = 1.7320508
F32 = jnp.float32
BF16 = jnp.bfloat16
NN = (((1,), (0,)), ((), ()))
NT = (((1,), (1,)), ((), ()))


def dot(a, b, dims=NN):
    return lax.dot_general(a, b, dims, preferred_element_type=F32)


def split3(x):
    hi = x.astype(BF16)
    rest = x - hi.astype(F32)
    mid = rest.astype(BF16)
    low = (rest - mid.astype(F32)).astype(BF16)
    return jnp.concatenate([hi.astype(F32), mid.astype(F32), low.astype(F32)], axis=0).astype(BF16)


def join3(y):
    rows = y.shape[0] // 3
    return y[:rows] + (y[rows : 2 * rows] + y[2 * rows :])


def tree_levels(leaves):
    levels = [leaves]
    while len(levels[-1]) > 1:
        last = levels[-1]
        levels.append([last[2 * i] + last[2 * i + 1] for i in range(len(last) // 2)])
    return levels


def cg_kernel(
    n,
    cross,
    total,
    rhs_ref,
    points_ref,
    basis_ref,
    order_ref,
    scale_ref,
    solution_ref,
    residual_ref,
    tiles,
    picks,
    sums,
    scalars,
    send_sem,
    recv_sem,
):
    me = lax.axis_index("leaf")
    rows, span = rhs_ref.shape
    count = span // LEAF
    upper = cross * K
    width = sums.shape[-1]

    def partner(slot):
        other = me
        for b in range(cross):
            bit = (slot // 2**b) % 2
            mine = (me // 2**b) % 2
            other = other + bit * (1 - 2 * mine) * 2**b
        return other

    def each_partner(act):
        if n <= 8:
            for slot in range(1, n):
                act(slot)
        else:
            def step(slot, carry):
                act(slot)
                return carry
            lax.fori_loop(1, n, step, 0)

    def broadcast(buffer, at, sem):
        def act(slot):
            pltpu.make_async_remote_copy(
                src_ref=buffer.at[at, 0],
                dst_ref=buffer.at[at, slot],
                send_sem=send_sem.at[sem],
                recv_sem=recv_sem.at[sem],
                device_id={"leaf": partner(slot)},
                device_id_type=pl.DeviceIdType.MESH,
            ).start()
        each_partner(act)

    def arrived(buffer, at, sem):
        landed = buffer.at[at, pl.ds(1, n - 1)]
        pltpu.make_async_copy(landed, landed, recv_sem.at[sem]).wait()

    def left(buffer, at, sem):
        landed = buffer.at[at, pl.ds(1, n - 1)]
        pltpu.make_async_copy(landed, landed, send_sem.at[sem]).wait()

    barrier = pltpu.get_barrier_semaphore()

    def greet(slot):
        pl.semaphore_signal(
            barrier, inc=1, device_id={"leaf": partner(slot)}, device_id_type=pl.DeviceIdType.MESH
        )

    each_partner(greet)

    row_id = lax.broadcasted_iota(jnp.int32, (LEAF, LEAF), 0)
    right_parts = []
    for t in range(count):
        cols = slice(t * LEAF, (t + 1) * LEAF)
        wanted = order_ref[:, cols] % LEAF
        picks[t] = jnp.where(row_id == wanted, 1.0, 0.0).astype(BF16)
        right_parts.append(join3(dot(split3(rhs_ref[:, cols]), picks[t])))
    right = jnp.concatenate(right_parts, axis=1)

    def project_and_send(direction, it):
        low16 = direction.astype(BF16)
        wide = low16.astype(F32)
        both = jnp.concatenate([wide, direction - wide], axis=0).astype(BF16)
        sums[it, 0, :, :upper] = dot(both, basis_ref[:upper, :], NT)
        if it == 0:
            pl.semaphore_wait(barrier, n - 1)
        broadcast(sums, it, it)
        return low16

    low16 = project_and_send(right, 0)

    factor = ROOT_THREE / scale_ref[0]
    for t in range(count):
        cols = slice(t * LEAF, (t + 1) * LEAF)
        coords = points_ref[:, cols] * factor
        tall = jnp.transpose(
            jnp.concatenate([coords, jnp.zeros((5, LEAF), F32)], axis=0)
        )
        for c in range(LEAF // CHUNK):
            part = slice(c * CHUNK, (c + 1) * CHUNK)
            square = None
            for axis in range(3):
                offset = tall[part, axis : axis + 1] - coords[axis : axis + 1, :]
                term = offset * offset
                square = term if square is None else square + term
            scaled = jnp.sqrt(square)
            tiles[t, part, :] = ((1.0 + scaled) * jnp.exp(-scaled)).astype(BF16)

    lane = lax.broadcasted_iota(jnp.int32, (rows, width), 1)
    halves = 2 ** (total - cross - 1)
    half = span // halves
    lane128 = lax.broadcasted_iota(jnp.int32, (rows, 128), 1)

    iterate = jnp.zeros_like(right)
    remain = right
    direction = right
    norm_now = None
    for it in range(ITERS):
        near = jnp.concatenate(
            [dot(low16[:, t * LEAF : (t + 1) * LEAF], tiles[t]) for t in range(count)], axis=1
        )
        local = [
            dot(low16[:, h * half : (h + 1) * half], basis_ref[upper:, h * half : (h + 1) * half], NT)
            for h in range(halves)
        ]
        spread = []
        for h in range(halves):
            cuts = []
            for depth in range(total - cross):
                size = halves // 2**depth
                first = h // size * size
                whole = local[first]
                for other in range(first + 1, first + size):
                    whole = whole + local[other]
                cuts.append(whole[:, depth * K : (depth + 1) * K])
            node = jnp.concatenate(cuts, axis=1).astype(BF16)
            spread.append(dot(node, basis_ref[upper:, h * half : (h + 1) * half]))
        result = near + NOISE * direction + jnp.concatenate(spread, axis=1)
        mine = jnp.sum(direction * result, axis=1, keepdims=True)
        if it == 0:
            first_norm = jnp.sum(remain * remain, axis=1, keepdims=True)
            scalars[it, 0] = jnp.where(lane128 < 64, mine, first_norm)
        else:
            scalars[it, 0] = jnp.broadcast_to(mine, (rows, 128))
        broadcast(scalars, it, ITERS + it)

        arrived(sums, it, it)
        levels = tree_levels([sums[it, j] for j in range(n)])
        node = jnp.zeros((rows, width), F32)
        cover = jnp.zeros((rows, width), F32)
        for depth in range(cross):
            here = (lane >= depth * K) & (lane < (depth + 1) * K)
            nodes = levels[cross - depth]
            node = jnp.where(here, nodes[0][:rows], node)
            terms = [s[:rows].astype(BF16).astype(F32) * (s[:rows] + s[rows:]) for s in nodes]
            cover = jnp.where(here, tree_levels(terms)[-1][0], cover)
        result = result + dot(node[:, :upper].astype(BF16), basis_ref[:upper, :])
        cover = jnp.sum(cover, axis=1, keepdims=True)

        arrived(scalars, it, ITERS + it)
        gathered = tree_levels([scalars[it, j] for j in range(n)])[-1][0]
        curve = gathered[:, :1] + cover
        if it == 0:
            norm_now = gathered[:, 64:65]
        alpha = norm_now / curve
        remain = remain - alpha * result
        if it + 1 < ITERS:
            at = ITERS + it
            scalars[at, 0] = jnp.broadcast_to(
                jnp.sum(remain * remain, axis=1, keepdims=True), (rows, 128)
            )
            broadcast(scalars, at, ITERS + at)
            iterate = iterate + alpha * direction
            arrived(scalars, at, ITERS + at)
            norm_next = tree_levels([scalars[at, j] for j in range(n)])[-1][0][:, :1]
            direction = remain + norm_next / norm_now * direction
            norm_now = norm_next
            low16 = project_and_send(direction, it + 1)
        else:
            iterate = iterate + alpha * direction

    for t in range(count):
        cols = slice(t * LEAF, (t + 1) * LEAF)
        both = jnp.concatenate([iterate[:, cols], remain[:, cols]], axis=0)
        placed = join3(dot(split3(both), picks[t], NT))
        solution_ref[:, cols] = placed[:rows]
        residual_ref[:, cols] = placed[rows:]
    for it in range(ITERS):
        left(sums, it, it)
    for at in range(2 * ITERS - 1):
        left(scalars, at, ITERS + at)


def body(rhs, points, basis, tree_order, lengthscale):
    rows, span = rhs.shape
    n = lax.axis_size("leaf")
    cross = n.bit_length() - 1
    total = basis.shape[0] // K
    width = -(-cross * K // 128) * 128
    vmem = pl.BlockSpec(memory_space=pltpu.VMEM)
    rounds = 3 * ITERS - 1
    return pl.pallas_call(
        functools.partial(cg_kernel, n, cross, total),
        out_shape=[jax.ShapeDtypeStruct((rows, span), F32)] * 2,
        in_specs=[vmem, vmem, vmem, vmem, pl.BlockSpec(memory_space=pltpu.SMEM)],
        out_specs=[vmem, vmem],
        scratch_shapes=[
            pltpu.VMEM((span // LEAF, LEAF, LEAF), BF16),
            pltpu.VMEM((span // LEAF, LEAF, LEAF), BF16),
            pltpu.VMEM((ITERS, n, 2 * rows, width), F32),
            pltpu.VMEM((2 * ITERS - 1, n, rows, 128), F32),
            pltpu.SemaphoreType.DMA((rounds,)),
            pltpu.SemaphoreType.DMA((rounds,)),
        ],
        compiler_params=pltpu.CompilerParams(
            collective_id=0, has_side_effects=True, vmem_limit_bytes=48 * 2**20
        ),
        name="cg",
    )(rhs, points, basis, tree_order.reshape(1, span), lengthscale)


def solution(mesh):
    in_specs = (
        P("probe", ("groups", "leaf")),
        P(None, ("groups", "leaf")),
        P(None, ("groups", "leaf")),
        P(("groups", "leaf")),
        P("groups"),
    )
    out_specs = (P("probe", ("groups", "leaf")), P("probe", ("groups", "leaf")))
    return jax.shard_map(body, mesh=mesh, in_specs=in_specs, out_specs=out_specs, check_vma=False)
```

time: 342 us -> 51.2 us (0.15)
  blocking collectives: 262 us -> 0 us
  Pallas kernels: 0 us -> 44.8 us
  local copies, waits for them, and re-layouts: 32.8 us -> 4.86 us
  matrix products: 26.6 us -> 0 us
  other arithmetic: 17.9 us -> 0 us
    psum x7 -> x0, blocking collectives: 134 us -> none  [the longest x4 75.2 us: squares(): return lax.psum(jnp.sum(remain * remain, axis=1, keepdims=True), 'leaf')]
    all_gather x4 -> x0, blocking collectives: 128 us -> none  [body(): piece = lax.all_gather(part_sums[None], 'leaf', axis=0, tiled=True)]
    pallas_call x0 -> x1, Pallas kernels: none -> 44.8 us  [body(): pl.pallas_call(functools.partial(cg_kernel, n, cross, total), out_shape=[...]
    dot_general x24 -> x0, matrix products: 26.6 us -> none  [the longest x8 13.9 us: body(): jnp.einsum('rmk,kmn->rmn', local_low, factor, preferred_element_type=jnp....]
    scatter x2 -> x0, local copies, waits for them, and re-layouts: 11.7 us -> none  [the longest x1 5.85 us: body(): residual = jnp.zeros_like(remain).at[:, local_order].set(remain)]
    reduce_sum x4 -> x0, other arithmetic: 7.18 us -> none  [the longest x3 5.24 us: squares(): return lax.psum(jnp.sum(remain * remain, axis=1, keepdims=True), 'leaf')]
    convert_element_type x4 -> x0, other arithmetic: 5.87 us -> none  [the longest x3 4.04 us: body(): operate_low16 = direction.astype(jnp.bfloat16)]
    gather x2 -> x0, local copies, waits for them, and re-layouts: 5.76 us -> none  [body(): right = jnp.take(rhs, local_order, axis=1)]
where the time goes in v1:
time: 51.2 us; the launch traced here: 50.9 us
  Pallas kernels  44.8 us (88%)
  local copies, waits for them, and re-layouts  4.86 us (9%)
  between operations  1.3 us (3%)
    pallas_call x1, Pallas kernels, body(): pl.pallas_call(functools.partial(cg_kernel, n, cross, total), out_shape=[...  44.8 us
    unnamed x10, local copies, waits for them, and re-layouts  4.86 us

profile of v1, /device:TPU:0, one launch (start us, length us, event | category | flops | bytes accessed | tf_op | source)
XLA Modules:
  0.0 50.9 jit_solution(15991825747152838992)
XLA Ops:
  1.3 0.0 copy-start
  1.3 1.3 %copy-done = bf16[320,2048]{1,0:T(8,128)(2,1)S(1)} copy-done((bf16[320,2048]{1,0:T(8,128)(2,1)S(1)}, bf16[320,2048]{1,0:T(8,128)(2,1)}, u32[]{:S(2)}) %copy-start) | copy-done | bytes 1310744
  2.6 0.0 copy-start.1
  2.6 0.8 %copy-done.1 = f32[8,2048]{1,0:T(8,128)S(1)} copy-done((f32[8,2048]{1,0:T(8,128)S(1)}, f32[8,2048]{1,0:T(8,128)}, u32[]{:S(2)}) %copy-start.1) | copy-done | bytes 65560
  3.4 0.0 copy-start.2
  3.4 0.8 %copy-done.2 = f32[3,2048]{1,0:T(4,128)S(1)} copy-done((f32[3,2048]{1,0:T(4,128)S(1)}, f32[3,2048]{1,0:T(4,128)}, u32[]{:S(2)}) %copy-start.2) | copy-done | bytes 24600
  4.2 0.0 copy-start.3
  4.2 0.7 %copy-done.3 = s32[2048]{0:T(1024)S(1)} copy-done((s32[2048]{0:T(1024)S(1)}, s32[2048]{0:T(1024)}, u32[]{:S(2)}) %copy-start.3) | copy-done | bytes 8216
  4.9 44.8 %cg.1 = (f32[8,2048]{1,0:T(8,128)S(1)}, f32[8,2048]{1,0:T(8,128)S(1)}) custom-call(f32[8,2048]{1,0:T(8,128)S(1)} %copy-done.1, f32[3,2048]{1,0:T(4,128)S(1)} %copy-done.2, bf16[320,2048]{1,0:T(8,128)(2,1)S(1)} %copy-done, s32[1,2048]{1,0:T(1,128)S(1)} %bitcast.1, f32[1]{0:T(128)S(6)} %copy.9.scale_ref), custom_call_target="tpu_custom_call" | custom-call | tf_op jit(solution)/shard_map/cg/pallas_call | solution.py:250
  49.7 0.6 %copy.10 = f32[8,2048]{1,0:T(8,128)} copy(f32[8,2048]{1,0:T(8,128)S(1)} %get-tuple-element.4) | data formatting | bytes 131072
  50.3 0.6 %copy.11 = f32[8,2048]{1,0:T(8,128)} copy(f32[8,2048]{1,0:T(8,128)S(1)} %get-tuple-element.5) | data formatting | bytes 131072
Async XLA Ops:
  1.3 1.3 %copy-start = (bf16[320,2048]{1,0:T(8,128)(2,1)S(1)}, bf16[320,2048]{1,0:T(8,128)(2,1)}, u32[]{:S(2)}) copy-start(bf16[320,2048]{1,0:T(8,128)(2,1)} %basis_ref.1) | copy-start | bytes 3932164
  2.6 0.8 %copy-start.1 = (f32[8,2048]{1,0:T(8,128)S(1)}, f32[8,2048]{1,0:T(8,128)}, u32[]{:S(2)}) copy-start(f32[8,2048]{1,0:T(8,128)} %rhs_ref.1) | copy-start | bytes 196612
  3.4 0.8 %copy-start.2 = (f32[3,2048]{1,0:T(4,128)S(1)}, f32[3,2048]{1,0:T(4,128)}, u32[]{:S(2)}) copy-start(f32[3,2048]{1,0:T(4,128)} %points_ref.1) | copy-start | bytes 73732
  4.2 0.7 %copy-start.3 = (s32[2048]{0:T(1024)S(1)}, s32[2048]{0:T(1024)}, u32[]{:S(2)}) copy-start(s32[2048]{0:T(1024)} %param.8) | copy-start | bytes 24580

commit v2 on v1

--- a/solution.py
+++ b/solution.py
@@ -60,10 +60,14 @@
     picks,
     sums,
     scalars,
+    gram,
+    forms,
     send_sem,
     recv_sem,
 ):
     me = lax.axis_index("leaf")
+    core = lax.axis_index("probe")
+    fused = gram is not None
     rows, span = rhs_ref.shape
     count = span // LEAF
     upper = cross * K
@@ -115,6 +119,10 @@
         )
 
     each_partner(greet)
+    if fused:
+        pl.semaphore_signal(
+            barrier, inc=1, device_id={"probe": 1 - core}, device_id_type=pl.DeviceIdType.MESH
+        )
 
     row_id = lax.broadcasted_iota(jnp.int32, (LEAF, LEAF), 0)
     right_parts = []
@@ -131,11 +139,70 @@
         both = jnp.concatenate([wide, direction - wide], axis=0).astype(BF16)
         sums[it, 0, :, :upper] = dot(both, basis_ref[:upper, :], NT)
         if it == 0:
-            pl.semaphore_wait(barrier, n - 1)
+            pl.semaphore_wait(barrier, n if fused else n - 1)
         broadcast(sums, it, it)
         return low16
 
     low16 = project_and_send(right, 0)
+
+    def swap(sem):
+        return pltpu.make_async_remote_copy(
+            src_ref=gram.at[core, pl.ds(1, n - 1)],
+            dst_ref=gram.at[core, pl.ds(1, n - 1)],
+            send_sem=send_sem.at[sem],
+            recv_sem=recv_sem.at[sem],
+            device_id={"probe": 1 - core},
+            device_id_type=pl.DeviceIdType.MESH,
+        )
+
+    gram_sem, swap_sem = 2 * ITERS, 2 * ITERS + 1
+    if fused:
+        square = dot(basis_ref[:upper, :], basis_ref[:upper, :], NT)
+        first = square[:K, :]
+        second = jnp.concatenate([square[K : 2 * K, K:], square[2 * K :, 2 * K :]], axis=1)
+        for h, block in enumerate((first, second)):
+            gram[h, 0, :K, :] = block[:, :128]
+            gram[h, 0, K:, :] = jnp.concatenate([block[: K // 2, 128:], block[K // 2 :, 128:]], axis=1)
+        for slot in range(1, n):
+            pltpu.make_async_remote_copy(
+                src_ref=gram.at[core, 0],
+                dst_ref=gram.at[core, slot],
+                send_sem=send_sem.at[gram_sem],
+                recv_sem=recv_sem.at[gram_sem],
+                device_id={"leaf": partner(slot)},
+                device_id_type=pl.DeviceIdType.MESH,
+            ).start()
+
+    def build_forms():
+        pairs = []
+        for p in range(n // 2):
+            rows_of = []
+            for h in range(2):
+                packed = gram[h, 2 * p] + gram[h, 2 * p + 1]
+                tail = jnp.concatenate([packed[K:, :K], packed[K:, K:]], axis=0)
+                rows_of.append(jnp.concatenate([packed[:K], tail], axis=1))
+            pairs.append(rows_of)
+        top = functools.reduce(jnp.maximum, [jnp.abs(block) for blocks in pairs for block in blocks])
+        top = jnp.max(jnp.max(top, axis=1, keepdims=True), axis=0, keepdims=True)
+        top = jnp.maximum(top, 1e-30)
+        turn = 1.0 / top
+        lane_k = lax.broadcasted_iota(jnp.int32, (K, upper), 1)
+        for p, (a, b) in enumerate(pairs):
+            none = jnp.zeros((K, K), F32)
+            grid = [
+                jnp.where(lane_k < K, a, 2.0 * a),
+                jnp.concatenate([none, b[:, :K], 2.0 * b[:, K : 2 * K]], axis=1),
+                jnp.concatenate([none, none, b[:, 2 * K :]], axis=1),
+            ]
+            whole = jnp.concatenate(grid, axis=0) * turn
+            hi = whole.astype(BF16)
+            rest = whole - hi.astype(F32)
+            mid = rest.astype(BF16)
+            low = (rest - mid.astype(F32)).astype(BF16)
+            forms[p, 0] = hi
+            forms[p, 1] = mid
+            forms[p, 2] = low
+        return top
 
     factor = ROOT_THREE / scale_ref[0]
     for t in range(count):
@@ -185,12 +252,38 @@
             spread.append(dot(node, basis_ref[upper:, h * half : (h + 1) * half]))
         result = near + NOISE * direction + jnp.concatenate(spread, axis=1)
         mine = jnp.sum(direction * result, axis=1, keepdims=True)
-        if it == 0:
+        more = it + 1 < ITERS
+        if fused:
+            parts = [mine, jnp.sum(remain * remain, axis=1, keepdims=True)]
+            message = jnp.zeros((rows, width), F32)
+            if more:
+                if it == 0:
+                    size = jnp.maximum(jnp.max(jnp.abs(result), axis=1, keepdims=True), 1e-30)
+                    shrink = 1.0 / size
+                unit = result * shrink
+                wide = unit.astype(BF16).astype(F32)
+                both = jnp.concatenate([wide, unit - wide], axis=0).astype(BF16)
+                seen = dot(both, basis_ref[:upper, :], NT)
+                seen = seen[:rows] + seen[rows:]
+                message = jnp.concatenate([seen, jnp.zeros((rows, width - upper), F32)], axis=1)
+                parts += [
+                    jnp.sum(unit * unit, axis=1, keepdims=True),
+                    mine if it == 0 else jnp.sum(remain * result, axis=1, keepdims=True),
+                    size,
+                ]
+            for i, part in enumerate(parts):
+                message = jnp.where(lane == upper + i, part, message)
+            scalars[it, 0] = message
+        elif it == 0:
             first_norm = jnp.sum(remain * remain, axis=1, keepdims=True)
             scalars[it, 0] = jnp.where(lane128 < 64, mine, first_norm)
         else:
             scalars[it, 0] = jnp.broadcast_to(mine, (rows, 128))
         broadcast(scalars, it, ITERS + it)
+        if fused and it == 0:
+            arrived_gram = gram.at[core, pl.ds(1, n - 1)]
+            pltpu.make_async_copy(arrived_gram, arrived_gram, recv_sem.at[gram_sem]).wait()
+            swap(swap_sem).start()
 
         arrived(sums, it, it)
         levels = tree_levels([sums[it, j] for j in range(n)])
@@ -204,6 +297,68 @@
             cover = jnp.where(here, tree_levels(terms)[-1][0], cover)
         result = result + dot(node[:, :upper].astype(BF16), basis_ref[:upper, :])
         cover = jnp.sum(cover, axis=1, keepdims=True)
+
+        if fused:
+            if more:
+                chains, turned = [], []
+                for p in range(n // 2):
+                    chain = jnp.zeros((rows, width), F32)
+                    full = jnp.zeros((rows, width), F32)
+                    for depth in range(cross):
+                        here = (lane >= depth * K) & (lane < (depth + 1) * K)
+                        at = levels[cross - depth][p // 2 ** (cross - 1 - depth)]
+                        chain = jnp.where(here, at[:rows].astype(BF16).astype(F32), chain)
+                        if p % 2 ** (cross - 1 - depth) == 0:
+                            full = jnp.where(here, at[:rows] + at[rows:], full)
+                    chains.append(chain)
+                    turned.append(full)
+                if it == 0:
+                    remain_cover = cover
+                else:
+                    moved = [now - ratio * old for now, old in zip(turned, turned_old)]
+                    terms = [chain * there for chain, there in zip(chains, moved)]
+                    remain_cover = jnp.sum(tree_levels(terms)[-1][0], axis=1, keepdims=True)
+                turned_old = turned
+                if it == 0:
+                    swap(swap_sem).wait_recv()
+                    form_top = build_forms()
+                terms = []
+                for p in range(n // 2):
+                    chain16 = chains[p][:, :upper].astype(BF16)
+                    image = dot(chain16, forms[p, 0]) + (
+                        dot(chain16, forms[p, 1]) + dot(chain16, forms[p, 2])
+                    )
+                    terms.append(image * chains[p][:, :upper])
+                form = jnp.sum(tree_levels(terms)[-1][0], axis=1, keepdims=True)
+
+            arrived(scalars, it, ITERS + it)
+            got = [scalars[it, j] for j in range(n)]
+            gathered = tree_levels(got)[-1][0]
+            curve = gathered[:, upper : upper + 1] + cover
+            norm_now = gathered[:, upper + 1 : upper + 2]
+            alpha = norm_now / curve
+            if more:
+                if it == 0:
+                    sizes = [row[:, upper + 4 : upper + 5] for row in got]
+                terms = []
+                for j in range(n):
+                    reach = alpha * sizes[j]
+                    factors = jnp.where(
+                        lane < upper,
+                        (2.0 * alpha) * chains[j // 2],
+                        jnp.where(lane == upper + 2, reach, 0.0),
+                    )
+                    terms.append(reach * (factors * got[j]))
+                spent = jnp.sum(tree_levels(terms)[-1][0], axis=1, keepdims=True)
+                crossed = alpha * (gathered[:, upper + 3 : upper + 4] + remain_cover)
+                norm_next = (norm_now - 2.0 * crossed) + (spent + (alpha * form_top) * (alpha * form))
+                ratio = norm_next / norm_now
+            iterate = iterate + alpha * direction
+            remain = remain - alpha * result
+            if more:
+                direction = remain + ratio * direction
+                low16 = project_and_send(direction, it + 1)
+            continue
 
         arrived(scalars, it, ITERS + it)
         gathered = tree_levels([scalars[it, j] for j in range(n)])[-1][0]
@@ -235,8 +390,12 @@
         residual_ref[:, cols] = placed[rows:]
     for it in range(ITERS):
         left(sums, it, it)
-    for at in range(2 * ITERS - 1):
+    for at in range(ITERS if fused else 2 * ITERS - 1):
         left(scalars, at, ITERS + at)
+    if fused:
+        sent = gram.at[core, pl.ds(1, n - 1)]
+        pltpu.make_async_copy(sent, sent, send_sem.at[gram_sem]).wait()
+        swap(swap_sem).wait_send()
 
 
 def body(rhs, points, basis, tree_order, lengthscale):
@@ -244,22 +403,31 @@
     n = lax.axis_size("leaf")
     cross = n.bit_length() - 1
     total = basis.shape[0] // K
-    width = -(-cross * K // 128) * 128
+    fused = n == 8
+    width = -(-(cross * K + 64) // 128) * 128
     vmem = pl.BlockSpec(memory_space=pltpu.VMEM)
     rounds = 3 * ITERS - 1
+
+    def kernel(*refs):
+        if not fused:
+            refs = refs[:11] + (None, None) + refs[11:]
+        cg_kernel(n, cross, total, *refs)
+
     return pl.pallas_call(
-        functools.partial(cg_kernel, n, cross, total),
+        kernel,
         out_shape=[jax.ShapeDtypeStruct((rows, span), F32)] * 2,
         in_specs=[vmem, vmem, vmem, vmem, pl.BlockSpec(memory_space=pltpu.SMEM)],
         out_specs=[vmem, vmem],
-        scratch_shapes=[
+        scratch_shapes=[shape for shape in [
             pltpu.VMEM((span // LEAF, LEAF, LEAF), BF16),
             pltpu.VMEM((span // LEAF, LEAF, LEAF), BF16),
             pltpu.VMEM((ITERS, n, 2 * rows, width), F32),
-            pltpu.VMEM((2 * ITERS - 1, n, rows, 128), F32),
+            pltpu.VMEM((ITERS, n, rows, width) if fused else (2 * ITERS - 1, n, rows, 128), F32),
+            pltpu.VMEM((2, n, K * 3 // 2, 128), F32) if fused else None,
+            pltpu.VMEM((n // 2, 3, cross * K, cross * K), BF16) if fused else None,
             pltpu.SemaphoreType.DMA((rounds,)),
             pltpu.SemaphoreType.DMA((rounds,)),
-        ],
+        ] if shape is not None],
         compiler_params=pltpu.CompilerParams(
             collective_id=0, has_side_effects=True, vmem_limit_bytes=48 * 2**20
         ),

time: 51.2 us -> 51.6 us (level)
  no operation moved by 1% of the time
where the time goes in v2:
time: 51.6 us; the launch traced here: 51.3 us
  Pallas kernels  45.1 us (87%)
  local copies, waits for them, and re-layouts  4.86 us (9%)
  between operations  1.3 us (3%)
    pallas_call x1, Pallas kernels, body(): pl.pallas_call(kernel, out_shape=[jax.ShapeDtypeStruct((rows, span), F32)...  45.1 us
    unnamed x10, local copies, waits for them, and re-layouts  4.86 us

profile of v2, /device:TPU:0, one launch (start us, length us, event | category | flops | bytes accessed | tf_op | source)
XLA Modules:
  0.0 51.3 jit_solution(13101484652597600376)
XLA Ops:
  1.3 0.0 copy-start
  1.3 1.3 %copy-done = bf16[320,2048]{1,0:T(8,128)(2,1)S(1)} copy-done((bf16[320,2048]{1,0:T(8,128)(2,1)S(1)}, bf16[320,2048]{1,0:T(8,128)(2,1)}, u32[]{:S(2)}) %copy-start) | copy-done | bytes 1310744
  2.6 0.0 copy-start.1
  2.6 0.8 %copy-done.1 = f32[8,2048]{1,0:T(8,128)S(1)} copy-done((f32[8,2048]{1,0:T(8,128)S(1)}, f32[8,2048]{1,0:T(8,128)}, u32[]{:S(2)}) %copy-start.1) | copy-done | bytes 65560
  3.4 0.0 copy-start.2
  3.4 0.8 %copy-done.2 = f32[3,2048]{1,0:T(4,128)S(1)} copy-done((f32[3,2048]{1,0:T(4,128)S(1)}, f32[3,2048]{1,0:T(4,128)}, u32[]{:S(2)}) %copy-start.2) | copy-done | bytes 24600
  4.2 0.0 copy-start.3
  4.2 0.7 %copy-done.3 = s32[2048]{0:T(1024)S(1)} copy-done((s32[2048]{0:T(1024)S(1)}, s32[2048]{0:T(1024)}, u32[]{:S(2)}) %copy-start.3) | copy-done | bytes 8216
  4.9 45.1 %cg.1 = (f32[8,2048]{1,0:T(8,128)S(1)}, f32[8,2048]{1,0:T(8,128)S(1)}) custom-call(f32[8,2048]{1,0:T(8,128)S(1)} %copy-done.1, f32[3,2048]{1,0:T(4,128)S(1)} %copy-done.2, bf16[320,2048]{1,0:T(8,128)(2,1)S(1)} %copy-done, s32[1,2048]{1,0:T(1,128)S(1)} %bitcast.1, f32[1]{0:T(128)S(6)} %copy.9.refs_4_), custom_call_target="tpu_custom_call" | custom-call | tf_op jit(solution)/shard_map/cg/pallas_call | solution.py:416
  50.0 0.6 %copy.10 = f32[8,2048]{1,0:T(8,128)} copy(f32[8,2048]{1,0:T(8,128)S(1)} %get-tuple-element.4) | data formatting | bytes 131072
  50.6 0.6 %copy.11 = f32[8,2048]{1,0:T(8,128)} copy(f32[8,2048]{1,0:T(8,128)S(1)} %get-tuple-element.5) | data formatting | bytes 131072
Async XLA Ops:
  1.3 1.3 %copy-start = (bf16[320,2048]{1,0:T(8,128)(2,1)S(1)}, bf16[320,2048]{1,0:T(8,128)(2,1)}, u32[]{:S(2)}) copy-start(bf16[320,2048]{1,0:T(8,128)(2,1)} %refs_2_.1) | copy-start | bytes 3932164
  2.6 0.8 %copy-start.1 = (f32[8,2048]{1,0:T(8,128)S(1)}, f32[8,2048]{1,0:T(8,128)}, u32[]{:S(2)}) copy-start(f32[8,2048]{1,0:T(8,128)} %refs_0_.1) | copy-start | bytes 196612
  3.4 0.8 %copy-start.2 = (f32[3,2048]{1,0:T(4,128)S(1)}, f32[3,2048]{1,0:T(4,128)}, u32[]{:S(2)}) copy-start(f32[3,2048]{1,0:T(4,128)} %refs_1_.1) | copy-start | bytes 73732
  4.2 0.7 %copy-start.3 = (s32[2048]{0:T(1024)S(1)}, s32[2048]{0:T(1024)}, u32[]{:S(2)}) copy-start(s32[2048]{0:T(1024)} %param.8) | copy-start | bytes 24580

commit v3 on v2

--- a/solution.py
+++ b/solution.py
@@ -49,10 +49,10 @@
     n,
     cross,
     total,
-    rhs_ref,
-    points_ref,
-    basis_ref,
-    order_ref,
+    rhs_hbm,
+    points_hbm,
+    basis_hbm,
+    order_hbm,
     scale_ref,
     solution_ref,
     residual_ref,
@@ -62,8 +62,13 @@
     scalars,
     gram,
     forms,
+    rhs_ref,
+    points_ref,
+    basis_ref,
+    order_ref,
     send_sem,
     recv_sem,
+    load_sem,
 ):
     me = lax.axis_index("leaf")
     core = lax.axis_index("probe")
@@ -111,6 +116,15 @@
         landed = buffer.at[at, pl.ds(1, n - 1)]
         pltpu.make_async_copy(landed, landed, send_sem.at[sem]).wait()
 
+    sources = (order_hbm, rhs_hbm, basis_hbm, points_hbm)
+    targets = (order_ref, rhs_ref, basis_ref, points_ref)
+    loads = [
+        pltpu.make_async_copy(source, target, load_sem.at[i])
+        for i, (source, target) in enumerate(zip(sources, targets))
+    ]
+    for load in loads:
+        load.start()
+
     barrier = pltpu.get_barrier_semaphore()
 
     def greet(slot):
@@ -124,6 +138,8 @@
             barrier, inc=1, device_id={"probe": 1 - core}, device_id_type=pl.DeviceIdType.MESH
         )
 
+    loads[0].wait()
+    loads[1].wait()
     row_id = lax.broadcasted_iota(jnp.int32, (LEAF, LEAF), 0)
     right_parts = []
     for t in range(count):
@@ -143,6 +159,7 @@
         broadcast(sums, it, it)
         return low16
 
+    loads[2].wait()
     low16 = project_and_send(right, 0)
 
     def swap(sem):
@@ -156,7 +173,8 @@
         )
 
     gram_sem, swap_sem = 2 * ITERS, 2 * ITERS + 1
-    if fused:
+
+    def send_gram():
         square = dot(basis_ref[:upper, :], basis_ref[:upper, :], NT)
         first = square[:K, :]
         second = jnp.concatenate([square[K : 2 * K, K:], square[2 * K :, 2 * K :]], axis=1)
@@ -204,6 +222,7 @@
             forms[p, 2] = low
         return top
 
+    loads[3].wait()
     factor = ROOT_THREE / scale_ref[0]
     for t in range(count):
         cols = slice(t * LEAF, (t + 1) * LEAF)
@@ -253,13 +272,13 @@
         result = near + NOISE * direction + jnp.concatenate(spread, axis=1)
         mine = jnp.sum(direction * result, axis=1, keepdims=True)
         more = it + 1 < ITERS
-        if fused:
+        whole_first = fused and it == 0
+        if whole_first:
+            pass
+        elif fused:
             parts = [mine, jnp.sum(remain * remain, axis=1, keepdims=True)]
             message = jnp.zeros((rows, width), F32)
             if more:
-                if it == 0:
-                    size = jnp.maximum(jnp.max(jnp.abs(result), axis=1, keepdims=True), 1e-30)
-                    shrink = 1.0 / size
                 unit = result * shrink
                 wide = unit.astype(BF16).astype(F32)
                 both = jnp.concatenate([wide, unit - wide], axis=0).astype(BF16)
@@ -268,8 +287,7 @@
                 message = jnp.concatenate([seen, jnp.zeros((rows, width - upper), F32)], axis=1)
                 parts += [
                     jnp.sum(unit * unit, axis=1, keepdims=True),
-                    mine if it == 0 else jnp.sum(remain * result, axis=1, keepdims=True),
-                    size,
+                    jnp.sum(remain * result, axis=1, keepdims=True),
                 ]
             for i, part in enumerate(parts):
                 message = jnp.where(lane == upper + i, part, message)
@@ -279,8 +297,9 @@
             scalars[it, 0] = jnp.where(lane128 < 64, mine, first_norm)
         else:
             scalars[it, 0] = jnp.broadcast_to(mine, (rows, 128))
-        broadcast(scalars, it, ITERS + it)
-        if fused and it == 0:
+        if not whole_first:
+            broadcast(scalars, it, ITERS + it)
+        if fused and it == 1:
             arrived_gram = gram.at[core, pl.ds(1, n - 1)]
             pltpu.make_async_copy(arrived_gram, arrived_gram, recv_sem.at[gram_sem]).wait()
             swap(swap_sem).start()
@@ -297,6 +316,23 @@
             cover = jnp.where(here, tree_levels(terms)[-1][0], cover)
         result = result + dot(node[:, :upper].astype(BF16), basis_ref[:upper, :])
         cover = jnp.sum(cover, axis=1, keepdims=True)
+        if whole_first:
+            size = jnp.maximum(jnp.max(jnp.abs(result), axis=1, keepdims=True), 1e-30)
+            shrink = 1.0 / size
+            unit = result * shrink
+            message = jnp.zeros((rows, width), F32)
+            for i, part in enumerate(
+                [
+                    jnp.sum(direction * result, axis=1, keepdims=True),
+                    jnp.sum(remain * remain, axis=1, keepdims=True),
+                    jnp.sum(unit * unit, axis=1, keepdims=True),
+                    size,
+                ]
+            ):
+                message = jnp.where(lane == upper + i, part, message)
+            scalars[it, 0] = message
+            broadcast(scalars, it, ITERS + it)
+            send_gram()
 
         if fused:
             if more:
@@ -312,34 +348,42 @@
                             full = jnp.where(here, at[:rows] + at[rows:], full)
                     chains.append(chain)
                     turned.append(full)
-                if it == 0:
-                    remain_cover = cover
-                else:
+                if it > 0:
                     moved = [now - ratio * old for now, old in zip(turned, turned_old)]
                     terms = [chain * there for chain, there in zip(chains, moved)]
                     remain_cover = jnp.sum(tree_levels(terms)[-1][0], axis=1, keepdims=True)
                 turned_old = turned
-                if it == 0:
+                if it == 1:
                     swap(swap_sem).wait_recv()
                     form_top = build_forms()
-                terms = []
-                for p in range(n // 2):
-                    chain16 = chains[p][:, :upper].astype(BF16)
-                    image = dot(chain16, forms[p, 0]) + (
-                        dot(chain16, forms[p, 1]) + dot(chain16, forms[p, 2])
-                    )
-                    terms.append(image * chains[p][:, :upper])
-                form = jnp.sum(tree_levels(terms)[-1][0], axis=1, keepdims=True)
+                if it > 0:
+                    terms = []
+                    for p in range(n // 2):
+                        chain16 = chains[p][:, :upper].astype(BF16)
+                        image = dot(chain16, forms[p, 0]) + (
+                            dot(chain16, forms[p, 1]) + dot(chain16, forms[p, 2])
+                        )
+                        terms.append(image * chains[p][:, :upper])
+                    form = jnp.sum(tree_levels(terms)[-1][0], axis=1, keepdims=True)
 
             arrived(scalars, it, ITERS + it)
             got = [scalars[it, j] for j in range(n)]
             gathered = tree_levels(got)[-1][0]
-            curve = gathered[:, upper : upper + 1] + cover
+            curve = gathered[:, upper : upper + 1]
+            if it > 0:
+                curve = curve + cover
             norm_now = gathered[:, upper + 1 : upper + 2]
             alpha = norm_now / curve
-            if more:
-                if it == 0:
-                    sizes = [row[:, upper + 4 : upper + 5] for row in got]
+            if more and it == 0:
+                sizes = [row[:, upper + 3 : upper + 4] for row in got]
+                terms = []
+                for j in range(n):
+                    reach = alpha * sizes[j]
+                    terms.append(reach * (reach * got[j][:, upper + 2 : upper + 3]))
+                spent = tree_levels(terms)[-1][0]
+                norm_next = (norm_now - 2.0 * (alpha * curve)) + spent
+                ratio = norm_next / norm_now
+            elif more:
                 terms = []
                 for j in range(n):
                     reach = alpha * sizes[j]
@@ -406,6 +450,7 @@
     fused = n == 8
     width = -(-(cross * K + 64) // 128) * 128
     vmem = pl.BlockSpec(memory_space=pltpu.VMEM)
+    hbm = pl.BlockSpec(memory_space=pltpu.MemorySpace.HBM)
     rounds = 3 * ITERS - 1
 
     def kernel(*refs):
@@ -416,7 +461,7 @@
     return pl.pallas_call(
         kernel,
         out_shape=[jax.ShapeDtypeStruct((rows, span), F32)] * 2,
-        in_specs=[vmem, vmem, vmem, vmem, pl.BlockSpec(memory_space=pltpu.SMEM)],
+        in_specs=[hbm, hbm, hbm, hbm, pl.BlockSpec(memory_space=pltpu.SMEM)],
         out_specs=[vmem, vmem],
         scratch_shapes=[shape for shape in [
             pltpu.VMEM((span // LEAF, LEAF, LEAF), BF16),
@@ -425,11 +470,16 @@
             pltpu.VMEM((ITERS, n, rows, width) if fused else (2 * ITERS - 1, n, rows, 128), F32),
             pltpu.VMEM((2, n, K * 3 // 2, 128), F32) if fused else None,
             pltpu.VMEM((n // 2, 3, cross * K, cross * K), BF16) if fused else None,
+            pltpu.VMEM((rows, span), F32),
+            pltpu.VMEM((3, span), F32),
+            pltpu.VMEM(basis.shape, BF16),
+            pltpu.VMEM((1, span), jnp.int32),
             pltpu.SemaphoreType.DMA((rounds,)),
             pltpu.SemaphoreType.DMA((rounds,)),
+            pltpu.SemaphoreType.DMA((4,)),
         ] if shape is not None],
         compiler_params=pltpu.CompilerParams(
-            collective_id=0, has_side_effects=True, vmem_limit_bytes=48 * 2**20
+            collective_id=0, has_side_effects=True, vmem_limit_bytes=63 * 2**20
         ),
         name="cg",
     )(rhs, points, basis, tree_order.reshape(1, span), lengthscale)

time: 51.6 us -> 48.7 us (0.944)
  local copies, waits for them, and re-layouts: 4.86 us -> 2.95 us
  Pallas kernels: 45.1 us -> 44.2 us
    unnamed x10 -> x2, local copies, waits for them, and re-layouts: 4.86 us -> 2.95 us
    pallas_call x1, Pallas kernels: 45.1 us -> 44.2 us  [body(): pl.pallas_call(kernel, out_shape=[jax.ShapeDtypeStruct((rows, span), F32)...]
where the time goes in v3:
time: 48.7 us; the launch traced here: 48.4 us
  Pallas kernels  44.2 us (91%)
  local copies, waits for them, and re-layouts  2.95 us (6%)
  between operations  1.29 us (3%)
    pallas_call x1, Pallas kernels, body(): pl.pallas_call(kernel, out_shape=[jax.ShapeDtypeStruct((rows, span), F32)...  44.2 us
    unnamed x2, local copies, waits for them, and re-layouts  2.95 us

profile of v3, /device:TPU:0, one launch (start us, length us, event | category | flops | bytes accessed | tf_op | source)
XLA Modules:
  0.0 48.4 jit_solution(12141041907136079985)
XLA Ops:
  1.3 44.2 %cg.1 = (f32[8,2048]{1,0:T(8,128)}, f32[8,2048]{1,0:T(8,128)}) custom-call(f32[8,2048]{1,0:T(8,128)} %refs_0_.1, f32[3,2048]{1,0:T(4,128)} %refs_1_.1, bf16[320,2048]{1,0:T(8,128)(2,1)} %refs_2_.1, s32[1,2048]{1,0:T(1,128)} %bitcast.1, f32[1]{0:T(128)S(6)} %copy.9.refs_4_), custom_call_target="tpu_custom_call" | custom-call | tf_op jit(solution)/shard_map/cg/pallas_call | solution.py:461
  45.5 1.5 %copy.10 = f32[8,2048]{1,0:T(8,128)} copy(f32[8,2048]{1,0:T(8,128)} %get-tuple-element.4) | data formatting | bytes 131072
  46.9 1.5 %copy.11 = f32[8,2048]{1,0:T(8,128)} copy(f32[8,2048]{1,0:T(8,128)} %get-tuple-element.5) | data formatting | bytes 131072

commit v4 on v3

--- a/solution.py
+++ b/solution.py
@@ -61,6 +61,8 @@
     sums,
     scalars,
     gram,
+    gram_own,
+    gram_inbox,
     forms,
     rhs_ref,
     points_ref,
@@ -162,41 +164,52 @@
     loads[2].wait()
     low16 = project_and_send(right, 0)
 
-    def swap(sem):
+    side = me % 2
+
+    def gram_copy(step, source, target, device):
         return pltpu.make_async_remote_copy(
-            src_ref=gram.at[core, pl.ds(1, n - 1)],
-            dst_ref=gram.at[core, pl.ds(1, n - 1)],
-            send_sem=send_sem.at[sem],
-            recv_sem=recv_sem.at[sem],
-            device_id={"probe": 1 - core},
+            src_ref=source,
+            dst_ref=target,
+            send_sem=send_sem.at[2 * ITERS + step],
+            recv_sem=recv_sem.at[2 * ITERS + step],
+            device_id=device,
             device_id_type=pl.DeviceIdType.MESH,
         )
 
-    gram_sem, swap_sem = 2 * ITERS, 2 * ITERS + 1
-
-    def send_gram():
+    def gram_first():
+        return gram_copy(0, gram_own.at[core, 1 - side], gram_inbox, {"leaf": partner(1)})
+
+    def gram_second(p):
+        return gram_copy(
+            1, gram.at[core, side, 0], gram.at[core, side, p], {"leaf": partner(2 * p)}
+        )
+
+    def gram_third():
+        return gram_copy(2, gram.at[core, side], gram.at[core, side], {"leaf": partner(1)})
+
+    def gram_fourth():
+        return gram_copy(3, gram.at[core], gram.at[core], {"probe": 1 - core})
+
+    def gram_others():
+        return gram.at[core, side, pl.ds(1, n // 2 - 1)]
+
+    if fused:
         square = dot(basis_ref[:upper, :], basis_ref[:upper, :], NT)
         first = square[:K, :]
         second = jnp.concatenate([square[K : 2 * K, K:], square[2 * K :, 2 * K :]], axis=1)
         for h, block in enumerate((first, second)):
-            gram[h, 0, :K, :] = block[:, :128]
-            gram[h, 0, K:, :] = jnp.concatenate([block[: K // 2, 128:], block[K // 2 :, 128:]], axis=1)
-        for slot in range(1, n):
-            pltpu.make_async_remote_copy(
-                src_ref=gram.at[core, 0],
-                dst_ref=gram.at[core, slot],
-                send_sem=send_sem.at[gram_sem],
-                recv_sem=recv_sem.at[gram_sem],
-                device_id={"leaf": partner(slot)},
-                device_id_type=pl.DeviceIdType.MESH,
-            ).start()
+            tail = jnp.concatenate([block[: K // 2, 128:], block[K // 2 :, 128:]], axis=1)
+            packed = jnp.concatenate([block[:, :128], tail], axis=0)
+            gram_own[h, 0] = packed[:48]
+            gram_own[h, 1] = packed[48:]
+        gram_first().start()
 
     def build_forms():
         pairs = []
         for p in range(n // 2):
             rows_of = []
             for h in range(2):
-                packed = gram[h, 2 * p] + gram[h, 2 * p + 1]
+                packed = jnp.concatenate([gram[h, 0, p], gram[h, 1, p]], axis=0)
                 tail = jnp.concatenate([packed[K:, :K], packed[K:, K:]], axis=0)
                 rows_of.append(jnp.concatenate([packed[:K], tail], axis=1))
             pairs.append(rows_of)
@@ -240,6 +253,12 @@
             scaled = jnp.sqrt(square)
             tiles[t, part, :] = ((1.0 + scaled) * jnp.exp(-scaled)).astype(BF16)
 
+    if fused:
+        gram_first().wait_recv()
+        gram[core, side, 0] = gram_own[core, side] + gram_inbox[...]
+        for p in range(1, n // 2):
+            gram_second(p).start()
+
     lane = lax.broadcasted_iota(jnp.int32, (rows, width), 1)
     halves = 2 ** (total - cross - 1)
     half = span // halves
@@ -250,6 +269,9 @@
     direction = right
     norm_now = None
     for it in range(ITERS):
+        if fused and it == 1:
+            gram_third().wait_recv()
+            gram_fourth().start()
         near = jnp.concatenate(
             [dot(low16[:, t * LEAF : (t + 1) * LEAF], tiles[t]) for t in range(count)], axis=1
         )
@@ -299,10 +321,6 @@
             scalars[it, 0] = jnp.broadcast_to(mine, (rows, 128))
         if not whole_first:
             broadcast(scalars, it, ITERS + it)
-        if fused and it == 1:
-            arrived_gram = gram.at[core, pl.ds(1, n - 1)]
-            pltpu.make_async_copy(arrived_gram, arrived_gram, recv_sem.at[gram_sem]).wait()
-            swap(swap_sem).start()
 
         arrived(sums, it, it)
         levels = tree_levels([sums[it, j] for j in range(n)])
@@ -332,7 +350,9 @@
                 message = jnp.where(lane == upper + i, part, message)
             scalars[it, 0] = message
             broadcast(scalars, it, ITERS + it)
-            send_gram()
+            others = gram_others()
+            pltpu.make_async_copy(others, others, recv_sem.at[2 * ITERS + 1]).wait()
+            gram_third().start()
 
         if fused:
             if more:
@@ -354,7 +374,7 @@
                     remain_cover = jnp.sum(tree_levels(terms)[-1][0], axis=1, keepdims=True)
                 turned_old = turned
                 if it == 1:
-                    swap(swap_sem).wait_recv()
+                    gram_fourth().wait_recv()
                     form_top = build_forms()
                 if it > 0:
                     terms = []
@@ -437,9 +457,11 @@
     for at in range(ITERS if fused else 2 * ITERS - 1):
         left(scalars, at, ITERS + at)
     if fused:
-        sent = gram.at[core, pl.ds(1, n - 1)]
-        pltpu.make_async_copy(sent, sent, send_sem.at[gram_sem]).wait()
-        swap(swap_sem).wait_send()
+        gram_first().wait_send()
+        others = gram_others()
+        pltpu.make_async_copy(others, others, send_sem.at[2 * ITERS + 1]).wait()
+        gram_third().wait_send()
+        gram_fourth().wait_send()
 
 
 def body(rhs, points, basis, tree_order, lengthscale):
@@ -451,11 +473,11 @@
     width = -(-(cross * K + 64) // 128) * 128
     vmem = pl.BlockSpec(memory_space=pltpu.VMEM)
     hbm = pl.BlockSpec(memory_space=pltpu.MemorySpace.HBM)
-    rounds = 3 * ITERS - 1
+    rounds = 3 * ITERS
 
     def kernel(*refs):
         if not fused:
-            refs = refs[:11] + (None, None) + refs[11:]
+            refs = refs[:11] + (None,) * 4 + refs[11:]
         cg_kernel(n, cross, total, *refs)
 
     return pl.pallas_call(
@@ -468,7 +490,9 @@
             pltpu.VMEM((span // LEAF, LEAF, LEAF), BF16),
             pltpu.VMEM((ITERS, n, 2 * rows, width), F32),
             pltpu.VMEM((ITERS, n, rows, width) if fused else (2 * ITERS - 1, n, rows, 128), F32),
-            pltpu.VMEM((2, n, K * 3 // 2, 128), F32) if fused else None,
+            pltpu.VMEM((2, 2, n // 2, K * 3 // 4, 128), F32) if fused else None,
+            pltpu.VMEM((2, 2, K * 3 // 4, 128), F32) if fused else None,
+            pltpu.VMEM((K * 3 // 4, 128), F32) if fused else None,
             pltpu.VMEM((n // 2, 3, cross * K, cross * K), BF16) if fused else None,
             pltpu.VMEM((rows, span), F32),
             pltpu.VMEM((3, span), F32),

time: 48.7 us -> 43.1 us (0.89)
  Pallas kernels: 44.2 us -> 38.6 us
    pallas_call x1, Pallas kernels: 44.2 us -> 38.6 us  [body(): pl.pallas_call(kernel, out_shape=[jax.ShapeDtypeStruct((rows, span), F32)...]
where the time goes in v4:
time: 43.1 us; the launch traced here: 42.8 us
  Pallas kernels  38.6 us (90%)
  local copies, waits for them, and re-layouts  2.95 us (7%)
  between operations  1.29 us (3%)
    pallas_call x1, Pallas kernels, body(): pl.pallas_call(kernel, out_shape=[jax.ShapeDtypeStruct((rows, span), F32)...  38.6 us
    unnamed x2, local copies, waits for them, and re-layouts  2.95 us

profile of v4, /device:TPU:0, one launch (start us, length us, event | category | flops | bytes accessed | tf_op | source)
XLA Modules:
  0.0 42.8 jit_solution(12817824597398999340)
XLA Ops:
  1.3 38.6 %cg.1 = (f32[8,2048]{1,0:T(8,128)}, f32[8,2048]{1,0:T(8,128)}) custom-call(f32[8,2048]{1,0:T(8,128)} %refs_0_.1, f32[3,2048]{1,0:T(4,128)} %refs_1_.1, bf16[320,2048]{1,0:T(8,128)(2,1)} %refs_2_.1, s32[1,2048]{1,0:T(1,128)} %bitcast.1, f32[1]{0:T(128)S(6)} %copy.9.refs_4_), custom_call_target="tpu_custom_call" | custom-call | tf_op jit(solution)/shard_map/cg/pallas_call | solution.py:483
  39.9 1.5 %copy.10 = f32[8,2048]{1,0:T(8,128)} copy(f32[8,2048]{1,0:T(8,128)} %get-tuple-element.4) | data formatting | bytes 131072
  41.4 1.5 %copy.11 = f32[8,2048]{1,0:T(8,128)} copy(f32[8,2048]{1,0:T(8,128)} %get-tuple-element.5) | data formatting | bytes 131072

commit v5 on v4

--- a/solution.py
+++ b/solution.py
@@ -54,8 +54,7 @@
     basis_hbm,
     order_hbm,
     scale_ref,
-    solution_ref,
-    residual_ref,
+    both_ref,
     tiles,
     picks,
     sums,
@@ -88,9 +87,14 @@
             other = other + bit * (1 - 2 * mine) * 2**b
         return other
 
+    known = [partner(slot) for slot in range(n)] if n <= 8 else None
+
+    def to(slot):
+        return known[slot] if known is not None else partner(slot)
+
     def each_partner(act):
         if n <= 8:
-            for slot in range(1, n):
+            for slot in ([6, 7, 4, 5, 2, 3, 1] if n == 8 else range(1, n)):
                 act(slot)
         else:
             def step(slot, carry):
@@ -105,7 +109,7 @@
                 dst_ref=buffer.at[at, slot],
                 send_sem=send_sem.at[sem],
                 recv_sem=recv_sem.at[sem],
-                device_id={"leaf": partner(slot)},
+                device_id={"leaf": to(slot)},
                 device_id_type=pl.DeviceIdType.MESH,
             ).start()
         each_partner(act)
@@ -131,7 +135,7 @@
 
     def greet(slot):
         pl.semaphore_signal(
-            barrier, inc=1, device_id={"leaf": partner(slot)}, device_id_type=pl.DeviceIdType.MESH
+            barrier, inc=1, device_id={"leaf": to(slot)}, device_id_type=pl.DeviceIdType.MESH
         )
 
     each_partner(greet)
@@ -177,15 +181,15 @@
         )
 
     def gram_first():
-        return gram_copy(0, gram_own.at[core, 1 - side], gram_inbox, {"leaf": partner(1)})
+        return gram_copy(0, gram_own.at[core, 1 - side], gram_inbox, {"leaf": to(1)})
 
     def gram_second(p):
         return gram_copy(
-            1, gram.at[core, side, 0], gram.at[core, side, p], {"leaf": partner(2 * p)}
+            1, gram.at[core, side, 0], gram.at[core, side, p], {"leaf": to(2 * p)}
         )
 
     def gram_third():
-        return gram_copy(2, gram.at[core, side], gram.at[core, side], {"leaf": partner(1)})
+        return gram_copy(2, gram.at[core, side], gram.at[core, side], {"leaf": to(1)})
 
     def gram_fourth():
         return gram_copy(3, gram.at[core], gram.at[core], {"probe": 1 - core})
@@ -450,8 +454,7 @@
         cols = slice(t * LEAF, (t + 1) * LEAF)
         both = jnp.concatenate([iterate[:, cols], remain[:, cols]], axis=0)
         placed = join3(dot(split3(both), picks[t], NT))
-        solution_ref[:, cols] = placed[:rows]
-        residual_ref[:, cols] = placed[rows:]
+        both_ref[:, cols] = placed
     for it in range(ITERS):
         left(sums, it, it)
     for at in range(ITERS if fused else 2 * ITERS - 1):
@@ -477,14 +480,14 @@
 
     def kernel(*refs):
         if not fused:
-            refs = refs[:11] + (None,) * 4 + refs[11:]
+            refs = refs[:10] + (None,) * 4 + refs[10:]
         cg_kernel(n, cross, total, *refs)
 
-    return pl.pallas_call(
+    both = pl.pallas_call(
         kernel,
-        out_shape=[jax.ShapeDtypeStruct((rows, span), F32)] * 2,
+        out_shape=pltpu.VMEM((2 * rows, span), F32),
         in_specs=[hbm, hbm, hbm, hbm, pl.BlockSpec(memory_space=pltpu.SMEM)],
-        out_specs=[vmem, vmem],
+        out_specs=vmem,
         scratch_shapes=[shape for shape in [
             pltpu.VMEM((span // LEAF, LEAF, LEAF), BF16),
             pltpu.VMEM((span // LEAF, LEAF, LEAF), BF16),
@@ -507,6 +510,7 @@
         ),
         name="cg",
     )(rhs, points, basis, tree_order.reshape(1, span), lengthscale)
+    return both[:rows], both[rows:]
 
 
 def solution(mesh):

time: 43.1 us -> 39.2 us (0.910)
  local copies, waits for them, and re-layouts: 2.95 us -> 0.66 us
  Pallas kernels: 38.6 us -> 37.1 us
    unnamed x2 -> x0, local copies, waits for them, and re-layouts: 2.95 us -> none
    pallas_call x1, Pallas kernels: 38.6 us -> 37.1 us  [body(): pl.pallas_call(kernel, out_shape=pltpu.VMEM((2 * rows, span), F32), in_sp...]
    slice x0 -> x1, local copies, waits for them, and re-layouts: none -> 0.66 us  [body(): return (both[:rows], both[rows:])]
where the time goes in v5:
time: 39.2 us; the launch traced here: 39 us
  Pallas kernels  37.1 us (95%)
  between operations  1.29 us (3%)
  local copies, waits for them, and re-layouts  0.66 us (2%)
    pallas_call x1, Pallas kernels, body(): pl.pallas_call(kernel, out_shape=pltpu.VMEM((2 * rows, span), F32), in_sp...  37.1 us

profile of v5, /device:TPU:0, one launch (start us, length us, event | category | flops | bytes accessed | tf_op | source)
XLA Modules:
  0.0 39.0 jit_solution(14752997406440036532)
XLA Ops:
  1.3 37.1 %cg.1 = f32[16,2048]{1,0:T(8,128)S(1)} custom-call(f32[8,2048]{1,0:T(8,128)} %refs_0_.1, f32[3,2048]{1,0:T(4,128)} %refs_1_.1, bf16[320,2048]{1,0:T(8,128)(2,1)} %refs_2_.1, s32[1,2048]{1,0:T(1,128)} %bitcast.1, f32[1]{0:T(128)S(6)} %copy.7.refs_4_), custom_call_target="tpu_custom_call" | custom-call | tf_op jit(solution)/shard_map/cg/pallas_call | solution.py:486
  38.3 0.7 %fusion = (f32[8,2048]{1,0:T(8,128)}, f32[8,2048]{1,0:T(8,128)}) fusion(f32[16,2048]{1,0:T(8,128)S(1)} %cg.1), kind=kLoop, calls=%fused_computation | loop fusion | bytes 262144 | tf_op jit(solution)/shard_map/slice | solution.py:513

commit v6 on v5

--- a/solution.py
+++ b/solution.py
@@ -254,7 +254,7 @@
                 offset = tall[part, axis : axis + 1] - coords[axis : axis + 1, :]
                 term = offset * offset
                 square = term if square is None else square + term
-            scaled = jnp.sqrt(square)
+            scaled = square * lax.rsqrt(jnp.maximum(square, 1e-30))
             tiles[t, part, :] = ((1.0 + scaled) * jnp.exp(-scaled)).astype(BF16)
 
     if fused:

time: 39.2 us -> 39.9 us (1.018)
  Pallas kernels: 37.1 us -> 37.7 us
    pallas_call x1, Pallas kernels: 37.1 us -> 37.7 us  [body(): pl.pallas_call(kernel, out_shape=pltpu.VMEM((2 * rows, span), F32), in_sp...]
where the time goes in v6:
time: 39.9 us; the launch traced here: 39.6 us
  Pallas kernels  37.7 us (94%)
  between operations  1.29 us (3%)
  local copies, waits for them, and re-layouts  0.66 us (2%)
    pallas_call x1, Pallas kernels, body(): pl.pallas_call(kernel, out_shape=pltpu.VMEM((2 * rows, span), F32), in_sp...  37.7 us

profile of v6, /device:TPU:0, one launch (start us, length us, event | category | flops | bytes accessed | tf_op | source)
XLA Modules:
  0.0 39.6 jit_solution(3774021629836333557)
XLA Ops:
  1.3 37.7 %cg.1 = f32[16,2048]{1,0:T(8,128)S(1)} custom-call(f32[8,2048]{1,0:T(8,128)} %refs_0_.1, f32[3,2048]{1,0:T(4,128)} %refs_1_.1, bf16[320,2048]{1,0:T(8,128)(2,1)} %refs_2_.1, s32[1,2048]{1,0:T(1,128)} %bitcast.1, f32[1]{0:T(128)S(6)} %copy.7.refs_4_), custom_call_target="tpu_custom_call" | custom-call | tf_op jit(solution)/shard_map/cg/pallas_call | solution.py:486
  39.0 0.7 %fusion = (f32[8,2048]{1,0:T(8,128)}, f32[8,2048]{1,0:T(8,128)}) fusion(f32[16,2048]{1,0:T(8,128)S(1)} %cg.1), kind=kLoop, calls=%fused_computation | loop fusion | bytes 262144 | tf_op jit(solution)/shard_map/slice | solution.py:513
